TPU v7x, 768 devices: a whole 4x8x12 slice. The times are simulated.
768 devices in a mesh: clip: 16 (over z_lo, x), tile: 48 (over z_hi, y, core).
Axes of the slice: x: 4, y: 8, z: 12 (z_hi: 3, z_lo: 4; z = z_hi * 4 + z_lo), core: 2. Of those that a mesh axis runs over, the one named last changes fastest.
Arguments:
- clip_frames: bfloat16 [64, 96, 64, 128], P('clip', 'tile'), may hold values from -6 to 6
- conv_weight: bfloat16 [3, 3, 3, 128, 128], replicated, may hold values from -0.109375 to 0.109375
- conv_bias: float32 [128], replicated, may hold values from -3 to 3
- out_grad: bfloat16 [64, 96, 64, 128], P('clip', 'tile'), may hold values from -6 to 6
- prev_group: int32 [16], P('clip'), may hold values from -1 to 15, as said below
Outputs:
- conv_out: bfloat16 [64, 96, 64, 128], P('clip', 'tile')
- weight_grad: float32 [3, 3, 3, 128, 128], replicated
Inputs may be any that keep to these rules, and one draw needn't show every extreme that they name: `prev_group`: no two groups name the same previous group, and following previous groups from any group ends at -1 after at most 16 steps.
All inputs are finite; a program needn't handle non-finite values.
Results may differ from a plain program's by a relative error of at most 0.0042.
Values may be sent and summed in bfloat16 or wider, within the bound.
A program may use at most 32 MiB of HBM per device.

v0:
```python
import math

import jax
import jax.numpy as jnp
from jax import lax
from jax.sharding import PartitionSpec as P


def with_halo(cells, sides, width):
    for axis, dim in sides:
        count = lax.axis_size(axis)
        ends = count - 1
        head = lax.slice_in_dim(cells, 0, width, axis=dim)
        tail = lax.slice_in_dim(cells, cells.shape[dim] - width, cells.shape[dim], axis=dim)
        cells = jnp.concatenate(
            [
                lax.ppermute(tail, axis, [(i, (i + 1) % count) for i in range(ends)]),
                cells,
                lax.ppermute(head, axis, [((i + 1) % count, i) for i in range(ends)]),
            ],
            axis=dim,
        )
    return cells


def window_columns(active, frame_tap, row_tap, group_frames, tall_rows, wide_cells):
    slab = active[frame_tap : frame_tap + group_frames, row_tap : row_tap + tall_rows]
    columns = jnp.concatenate(
        [slab[:, :, shift_w : shift_w + wide_cells] for shift_w in range(3)], axis=-1
    )
    return columns.reshape(group_frames * tall_rows * wide_cells, columns.shape[-1])


def body(clip_frames, conv_weight, conv_bias, out_grad, prev_group):
    group_frames, tall_rows, wide_cells, chans = clip_frames.shape
    owner = prev_group[0]
    tail = clip_frames[group_frames - 2 :]
    shards = lax.all_gather(tail, "clip", axis=0, tiled=True)
    number = shards.shape[0] // 2
    blocks = shards.reshape((number, 2) + shards.shape[1:])
    group_ids = jnp.arange(number, dtype=jnp.int32)
    chosen = (group_ids == owner).reshape((number, 1, 1, 1, 1))
    cached = jnp.sum(jnp.where(chosen, blocks, jnp.zeros_like(blocks)), axis=0)
    joined = jnp.concatenate([cached, clip_frames], axis=0)
    joined = with_halo(joined, (("tile", 1),), 1)
    joined = jnp.pad(joined, ((0, 0), (0, 0), (1, 1), (0, 0)))
    active = jax.nn.silu(joined.astype(jnp.float32)).astype(jnp.bfloat16)
    weights = conv_weight.reshape(3, 3, 3 * chans, chans)
    grad_rows = out_grad.reshape(group_frames * tall_rows * wide_cells, chans)
    result = jnp.zeros((group_frames * tall_rows * wide_cells, chans), jnp.float32)
    grads = []
    for frame_tap in range(3):
        for row_tap in range(3):
            columns = window_columns(
                active, frame_tap, row_tap, group_frames, tall_rows, wide_cells
            )
            result = result + jnp.dot(
                columns, weights[frame_tap, row_tap], preferred_element_type=jnp.float32
            )
            grads.append(
                lax.dot_general(
                    columns, grad_rows, (((0,), (0,)), ((), ())), preferred_element_type=jnp.float32
                )
            )
    conv_out = (
        (result + conv_bias)
        .reshape(group_frames, tall_rows, wide_cells, chans)
        .astype(jnp.bfloat16)
    )
    local_terms = jnp.stack(grads, axis=0).reshape(27 * chans, chans)
    factor = 1.0 / math.sqrt(
        group_frames * lax.axis_size("clip") * tall_rows * lax.axis_size("tile") * wide_cells
    )
    summed = lax.psum(local_terms, ("clip", "tile"))
    weight_grad = (summed * factor).reshape(3, 3, 3, chans, chans)
    return (conv_out, weight_grad)


def solution(mesh):
    return jax.shard_map(
        body,
        mesh=mesh,
        in_specs=(
            P("clip", "tile", None, None),
            P(),
            P(),
            P("clip", "tile", None, None),
            P("clip"),
        ),
        out_specs=(P("clip", "tile", None, None), P()),
        check_vma=False,
    )
```

profile of v0, /device:TPU:1, one launch (start us, length us, event | category | flops | bytes accessed | tf_op | source)
XLA Modules:
  0.0 611.3 jit_solution(14425523854069688804)
XLA Ops:
  7.2 0.0 all-gather.2.cloned.1.call-start
  7.2 1.5 slice.153
  8.8 0.0 all-gather.2.cloned.1.call-update
  8.8 0.0 all-reduce.3.cloned.1.call-start
  9.5 85.6 %all-gather.2.cloned.1.call-done = bf16[32,2,64,128]{3,2,1,0:T(8,128)(2,1)} async-done(((bf16[2,2,64,128]{3,2,1,0:T(8,128)(2,1)}), bf16[32,2,64,128]{3,2,1,0:T(8,128)(2,1)}) %all-gather.2.cloned.1.call-update) | async-done | bytes 1048592 | tf_op jit(solution)/shard_map/all_gather | solution.py:38
  95.1 1.5 select_reduce_fusion
  96.6 0.9 fusion.19
  97.5 14.1 %collective-permute-start = (bf16[6,1,64,128]{3,2,1,0:T(8,128)(2,1)S(1)}, bf16[6,1,64,128]{3,2,1,0:T(8,128)(2,1)S(1)}, u32[]{:S(2)}, u32[]{:S(2)}) collective-permute-start(bf16[6,1,64,128]{3,2,1,0:T(8,128)(2,1)S(1)} %get-tuple-element.29), channel_id=1, source_target_pairs={{0,1},{1,2},{2,3},{3,4},{4,5},{5,6},{6,7},{7,8},{8,9},{9,10},{10,1... | collective-permute-start | bytes 294920 | tf_op jit(solution)/shard_map/ppermute | solution.py:17
  111.6 1.9 collective-permute-start.1
  113.5 4.0 collective-permute-done.1
  117.5 0.3 fusion.14
  117.8 0.2 fusion.22
  118.1 0.5 fusion.21
  118.7 0.3 fusion.10
  119.0 0.1 pad_maximum_fusion
  119.1 0.3 fusion.9
  119.5 0.3 fusion.8
  119.8 0.1 pad_maximum_fusion.2
  119.9 0.3 fusion.7
  120.2 0.3 fusion.6
  120.5 1.0 pad_maximum_fusion.4
  121.6 0.3 fusion.5
  121.9 0.3 fusion.4
  122.3 0.3 fusion.3
  122.6 0.3 fusion.2
  123.0 1.2 copy-done.1
  124.1 0.0 all-reduce.3.cloned.1.call-update
  124.2 1.2 fusion.20
  125.5 1.2 convolution_add_fusion.7
  126.6 0.3 convolution_add_fusion.6
  127.0 0.3 convolution_add_fusion.5
  127.3 0.3 convolution_add_fusion.4
  127.5 0.1 copy-done.2
  127.6 0.3 convolution_add_fusion.3
  127.9 0.0 copy-done.21
  127.9 0.0 copy-done.23
  127.9 0.1 pad_maximum_fusion.8
  128.0 0.0 copy-done.9
  128.0 0.0 copy-done.11
  128.1 0.0 copy-done.13
  128.1 0.0 copy-done.15
  128.2 0.0 copy-done.17
  128.2 0.1 pad_maximum_fusion.6
  128.3 0.3 convolution_add_fusion.2
  128.6 0.3 convolution_add_fusion.1
  128.8 0.9 fusion.1
  129.8 471.8 %all-reduce.3.cloned.1.call-done = f32[3456,128]{1,0:T(8,128)} async-done(((f32[3456,128]{1,0:T(8,128)}), f32[3456,128]{1,0:T(8,128)}) %all-reduce.3.cloned.1.call-update) | async-done | bytes 1769488 | tf_op jit(solution)/shard_map/psum | solution.py:74
  601.6 2.8 broadcast_multiply_fusion
  (43 shorter events, 0.1 us)
Async XLA Ops:
  7.2 111.5 %copy-start = (bf16[4,2,64,128]{3,2,1,0:T(8,128)(2,1)S(1)}, bf16[4,2,64,128]{3,2,1,0:T(8,128)(2,1)}, u32[]{:S(2)}) copy-start(bf16[4,2,64,128]{3,2,1,0:T(8,128)(2,1)} %param.8) | copy-start | bytes 393220
  7.2 110.3 %copy-start.5 = (bf16[4,2,64,128]{3,2,1,0:T(8,128)(2,1)S(1)}, bf16[4,2,64,128]{3,2,1,0:T(8,128)(2,1)}, u32[]{:S(2)}) copy-start(bf16[4,2,64,128]{3,2,1,0:T(8,128)(2,1)} %param.5) | copy-start | bytes 393220
  7.2 87.9 %all-gather.2.cloned.1.call-start = ((), (), s32[]{:S(2)}) async-start(), calls=%async_computation | async-start | bytes 1114112 | tf_op jit(solution)/shard_map/all_gather | solution.py:38
  8.8 592.8 %all-reduce.3.cloned.1.call-start = ((), (), s32[]{:S(2)}) async-start(), calls=%async_computation.1 | async-start | bytes 3538944 | tf_op jit(solution)/shard_map/psum | solution.py:74
  97.5 16.0 %collective-permute-start = (bf16[6,1,64,128]{3,2,1,0:T(8,128)(2,1)S(1)}, bf16[6,1,64,128]{3,2,1,0:T(8,128)(2,1)S(1)}, u32[]{:S(2)}, u32[]{:S(2)}) collective-permute-start(bf16[6,1,64,128]{3,2,1,0:T(8,128)(2,1)S(1)} %get-tuple-element.29), channel_id=1, source_target_pairs={{0,1},{1,2},{2,3},{3,4},{4,5},{5,6},{6,7},{7,8},{8,9},{9,10},{10,1... | collective-permute-start | bytes 294920 | tf_op jit(solution)/shard_map/ppermute | solution.py:17
  111.6 5.9 collective-permute-start.1
  118.6 3.3 copy-start.12
  118.6 3.3 copy-start.14
  118.6 3.3 copy-start.16
  118.6 3.6 copy-start.6
  118.6 3.6 copy-start.8
  118.7 3.6 copy-start.10
  118.7 3.9 copy-start.18
  118.7 3.9 copy-start.20
  118.7 3.9 copy-start.22
  122.9 1.2 copy-start.1
  124.2 2.5 copy-start.4
  124.2 3.1 copy-start.3
  126.6 1.0 copy-start.2
  126.9 1.0 copy-start.19
  126.9 1.0 copy-start.21
  126.9 1.0 copy-start.23
  126.9 1.1 copy-start.7
  126.9 1.1 copy-start.9
  127.0 1.1 copy-start.11
  127.0 1.1 copy-start.13
  127.0 1.2 copy-start.15
  127.0 1.2 copy-start.17
  128.2 0.7 copy-start.24
Sparse Core Ops, SparseCore 0:
  11.0 84.0 all-gather.1
  124.3 477.2 all-reduce.2
where the time goes:
time: 613 us; the launch traced here: 611 us
  waiting for transfers between devices  561 us (92%)
  starting transfers between devices  16.1 us (3%)
  between operations  15.2 us (2%)
  matrix products  7.72 us (1%)
  other arithmetic  6.95 us (1%)
    psum x1, waiting for transfers between devices, body(): summed = lax.psum(local_terms, ('clip', 'tile'))  472 us
    all_gather x1, waiting for transfers between devices, body(): shards = lax.all_gather(tail, 'clip', axis=0, tiled=True)  85.6 us
    ppermute x1, starting transfers between devices, with_halo(): lax.ppermute(tail, axis, [(i, (i + 1) % count) for i in range(ends)])  14.1 us
  transfers between devices with their start and end apart: 4, of which 3 were waited for; matrix products, arithmetic and copies ran while one was open for 1% of the time, Pallas kernels for 0%

commit v1 on v0

v1 whole, which is shorter than its diff:
```python
import functools
import math

import jax
import jax.numpy as jnp
from jax import lax
from jax.experimental import pallas as pl
from jax.experimental.pallas import tpu as pltpu
from jax.sharding import PartitionSpec as P

MESH = pl.DeviceIdType.MESH
NX, NZL, NZH, NY = 4, 4, 3, 8
NZ = NZH * NZL
F32, BF16 = jnp.float32, jnp.bfloat16


def sizes():
    half = 27 * 128 // 2
    part = half // NX
    slot = -(-part // (16 * NY)) * 16
    return half, part, slot


class Place:
    def __init__(self):
        clip, tile = lax.axis_index("clip"), lax.axis_index("tile")
        self.x, self.zl = clip % NX, clip // NX
        self.core, self.y, self.zh = tile % 2, (tile // 2) % NY, tile // (2 * NY)
        self.z = self.zh * NZL + self.zl
        self.clip, self.tile = clip, tile

    def at(self, x=None, y=None, z=None, core=None):
        x = self.x if x is None else x
        y = self.y if y is None else y
        z = self.z if z is None else z
        core = self.core if core is None else core
        return ((z % NZL) * NX + x, ((z // NZL) * NY + y) * 2 + core)


def kernel(
    factor, frames, weight, bias, grads, prev, out, gathered,
    act, cat, turned, gext, acc,
    ids_x, ids_z, gx, gm, gz, zx, zm, zz,
    local, core_out, core_in, sum_a, x_out, x_in, sum_b, y_out, y_in, z_buf,
    s_sem, r_sem,
):
    half, part, slot = sizes()
    me = Place()
    tiles = 2 * NY * NZH
    up, down = (me.tile + tiles - 1) % tiles, (me.tile + 1) % tiles
    other = 1 - me.core
    core_peer = me.at(core=other)
    diag_tile = jnp.where(me.core == 0, up, down)
    xs = [(me.x + j) % NX for j in range(1, NX)]
    ys = [(me.y + j) % NY for j in range(1, NY)]
    zs = [(me.z + j) % NZ for j in range(1, NZ)]
    zls = [(me.zl + j) % NZL for j in range(1, NZL)]
    x_peers = [me.at(x=x) for x in xs]
    y_peers = [me.at(y=y) for y in ys]
    z_peers = [me.at(z=z) for z in zs]
    zl_peers = [me.at(z=me.zh * NZL + zl) for zl in zls]

    barrier = pltpu.get_barrier_semaphore()
    everyone = [core_peer, (me.clip, diag_tile), *x_peers, *y_peers, *z_peers]
    for peer in everyone:
        pl.semaphore_signal(barrier, inc=1, device_id=peer, device_id_type=MESH)

    count = [0]
    started = []

    def send(src, dst, peer):
        k = count[0]
        count[0] += 1
        copy = pltpu.make_async_remote_copy(
            src_ref=src, dst_ref=dst, send_sem=s_sem.at[k], recv_sem=r_sem.at[k],
            device_id=peer, device_id_type=MESH,
        )
        copy.start()
        started.append(copy)
        return copy

    for s in range(4):
        v = frames[s].astype(F32)
        act[s, 1:3] = (v / (1.0 + jnp.exp(-v))).astype(BF16)
    own_id = jnp.full((8, 128), prev[0], jnp.int32)
    ids_x[me.x] = own_id
    ids_z[me.zl] = own_id
    gext[0:512] = grads[...].reshape(512, 128)
    pl.semaphore_wait(barrier, len(everyone))

    halo_up = send(act.at[:, 1], act.at[:, 3], (me.clip, up))
    halo_down = send(act.at[:, 2], act.at[:, 0], (me.clip, down))
    g_first = [send(gext.at[pl.ds(0, 256)], gx.at[me.x], peer) for peer in x_peers]
    id_x = [send(ids_x.at[me.x], ids_x.at[me.x], peer) for peer in x_peers]
    id_z = [send(ids_z.at[me.zl], ids_z.at[me.zl], peer) for peer in zl_peers]
    gx[me.x] = gext[0:256]

    halo_up.wait_recv()
    halo_down.wait_recv()
    top = jnp.where(me.tile == 0, 0.0, 1.0).astype(F32)
    bottom = jnp.where(me.tile == tiles - 1, 0.0, 1.0).astype(F32)

    row_at = lax.broadcasted_iota(jnp.int32, (64, 128), 0)

    def widen(s, _):
        for r in range(4):
            v = act[s, r].astype(F32)
            if r == 0:
                v = v * top
            if r == 3:
                v = v * bottom
            left = jnp.where(row_at == 0, 0.0, pltpu.roll(v, 1, 0))
            right = jnp.where(row_at == 63, 0.0, pltpu.roll(v, 63, 0))
            cat[s, r, :, 0:128] = left.astype(BF16)
            cat[s, r, :, 128:256] = v.astype(BF16)
            cat[s, r, :, 256:384] = right.astype(BF16)
        return 0

    lax.fori_loop(0, 4, widen, 0)

    def turn(s, b):
        for e in range(3):
            block = cat[s, pl.ds(b, 2), :, e * 128 : (e + 1) * 128].reshape(128, 128)
            start = pl.multiple_of((b * 3 + e) * 128, 128)
            turned[s, pl.ds(start, 128), :] = block.T

    for s in range(4):
        lax.fori_loop(0, 3, lambda b, _, s=s: (turn(s, b), 0)[1], 0)

    def grad_of(a):
        first = (2 - a) * 128

        def block(k, _):
            rows = pl.ds(pl.multiple_of(k * 384, 128), 384)
            total = jnp.zeros((384, 128), F32)
            for s in range(4):
                total = total + jnp.dot(
                    turned[s, rows, :], gext[first + s * 128 : first + (s + 1) * 128],
                    preferred_element_type=F32,
                )
            local[pl.ds(pl.multiple_of(a * 1152 + k * 384, 128), 384)] = total
            return 0

        lax.fori_loop(0, 3, block, 0)

    grad_of(2)

    for copy in g_first + id_x:
        copy.wait_recv()

    def pick(target, k):
        return (ids_x[k][0:1] == target * NX + me.x).astype(F32)

    def g_message(target):
        total = jnp.zeros((256, 128), F32)
        for k in range(NX):
            total = total + gx[k].astype(F32) * pick(target, k)
        return total.astype(BF16)

    g_second = []
    for j in range(1, NZL):
        gm[j] = g_message(zls[j - 1])
        g_second.append(send(gm.at[j], gz.at[j], zl_peers[j - 1]))
    gm[0] = g_message(me.zl)

    acc[...] = jnp.zeros((6, 128, 128), F32)

    def conv(a, _):
        for s in range(4):
            total = jnp.zeros((128, 128), F32)
            for b in range(3):
                total = total + jnp.dot(
                    cat[s, b : b + 2].reshape(128, 384), weight[a, b], preferred_element_type=F32
                )
            acc[s + 2 - a] = acc[s + 2 - a] + total
        return 0

    lax.fori_loop(0, 3, conv, 0)
    zx[me.x] = acc[4:6].reshape(256, 128).astype(BF16)
    z_first = [send(zx.at[me.x], zx.at[me.x], peer) for peer in x_peers]

    for copy in g_second:
        copy.wait_recv()
    gn = gm[0].astype(F32)
    for j in range(1, NZL):
        gn = gn + gz[j].astype(F32)
    gext[512:768] = gn.astype(BF16)
    grad_of(1)
    grad_of(0)

    start_other = pl.multiple_of(other * half, half)
    start_own = pl.multiple_of(me.core * half, half)
    core_out[...] = local[pl.ds(start_other, half)].astype(BF16)
    core_copy = send(core_out, core_in, core_peer)

    for copy in z_first + id_z:
        copy.wait_recv()

    def z_message(target):
        ids = ids_z[target][0:1]
        total = jnp.zeros((256, 128), F32)
        for k in range(NX):
            total = total + zx[k].astype(F32) * (ids == me.zl * NX + k).astype(F32)
        return total.astype(BF16)

    z_second = []
    for j in range(1, NZL):
        zm[j] = z_message(zls[j - 1])
        z_second.append(send(zm.at[j], zz.at[j], zl_peers[j - 1]))
    zm[0] = z_message(me.zl)

    core_copy.wait_recv()

    def add_core(k, _):
        rows = pl.ds(pl.multiple_of(k * part, 16), part)
        own = pl.ds(pl.multiple_of(start_own + k * part, 16), part)
        total = local[own] + core_in[rows].astype(F32)
        sum_a[rows] = total
        x_out[rows] = total.astype(BF16)
        return 0

    lax.fori_loop(0, NX, add_core, 0)

    x_copies = [
        send(x_out.at[pl.ds(pl.multiple_of(xs[j] * part, 16), part)], x_in.at[j], x_peers[j])
        for j in range(NX - 1)
    ]
    if NY * slot > part:
        y_out[pl.ds(part, NY * slot - part)] = jnp.zeros((NY * slot - part, 128), BF16)
        sum_b[pl.ds(part, NY * slot - part)] = jnp.zeros((NY * slot - part, 128), F32)
    for copy in x_copies:
        copy.wait_recv()
    total = sum_a[pl.ds(pl.multiple_of(me.x * part, 16), part)]
    for j in range(NX - 1):
        total = total + x_in[j].astype(F32)
    sum_b[0:part] = total
    y_out[0:part] = total.astype(BF16)

    y_copies = [
        send(y_out.at[pl.ds(pl.multiple_of(ys[j] * slot, 16), slot)], y_in.at[j], y_peers[j])
        for j in range(NY - 1)
    ]
    for copy in z_second:
        copy.wait_recv()
    zn = zm[0].astype(F32)
    for j in range(1, NZL):
        zn = zn + zz[j].astype(F32)
    acc[0:2] = acc[0:2] + zn.reshape(2, 128, 128)
    out[...] = (acc[0:4].reshape(512, 128) + bias[...]).astype(BF16).reshape(4, 2, 64, 128)

    for copy in y_copies:
        copy.wait_recv()
    total = sum_b[pl.ds(pl.multiple_of(me.y * slot, 16), slot)]
    for j in range(NY - 1):
        total = total + y_in[j].astype(F32)
    z_buf[me.z] = total.astype(BF16)

    z_copies = [send(z_buf.at[me.z], z_buf.at[me.z], peer) for peer in z_peers]
    for copy in z_copies:
        copy.wait_recv()
    total = z_buf[0].astype(F32)
    for k in range(1, NZ):
        total = total + z_buf[k].astype(F32)
    mine = pl.ds(pl.multiple_of(me.y * slot, 16), slot)
    gathered[me.core, me.x, mine] = (total * factor).astype(BF16)

    block = gathered.at[me.core, me.x, mine]
    for copy in [send(block, block, peer) for peer in y_peers]:
        copy.wait_recv()
    block = gathered.at[me.core, me.x]
    for copy in [send(block, block, peer) for peer in x_peers]:
        copy.wait_recv()
    block = gathered.at[me.core]
    send(block, block, core_peer).wait_recv()
    for copy in started:
        copy.wait_send()


def n_copies():
    return 2 + 5 * (NX - 1) + 3 * (NZL - 1) + 1 + 2 * (NY - 1) + (NZ - 1) + 1


def body(clip_frames, conv_weight, conv_bias, out_grad, prev_group):
    half, part, slot = sizes()
    factor = 1.0 / math.sqrt(
        4 * lax.axis_size("clip") * 2 * lax.axis_size("tile") * 64
    )
    vmem = pl.BlockSpec(memory_space=pltpu.VMEM)
    V = pltpu.VMEM
    n = n_copies()
    conv_out, gathered = pl.pallas_call(
        functools.partial(kernel, factor),
        out_shape=(
            jax.ShapeDtypeStruct((4, 2, 64, 128), BF16),
            jax.ShapeDtypeStruct((2, NX, NY * slot, 128), BF16),
        ),
        in_specs=[vmem, vmem, vmem, vmem, pl.BlockSpec(memory_space=pltpu.SMEM)],
        out_specs=(vmem, vmem),
        scratch_shapes=[
            V((4, 4, 64, 128), BF16),
            V((4, 4, 64, 384), BF16),
            V((4, 1152, 128), BF16),
            V((768, 128), BF16),
            V((6, 128, 128), F32),
            V((NX, 8, 128), jnp.int32),
            V((NZL, 8, 128), jnp.int32),
            V((NX, 256, 128), BF16),
            V((NZL, 256, 128), BF16),
            V((NZL, 256, 128), BF16),
            V((NX, 256, 128), BF16),
            V((NZL, 256, 128), BF16),
            V((NZL, 256, 128), BF16),
            V((3456, 128), F32),
            V((half, 128), BF16),
            V((half, 128), BF16),
            V((half, 128), F32),
            V((half, 128), BF16),
            V((NX - 1, part, 128), BF16),
            V((NY * slot, 128), F32),
            V((NY * slot, 128), BF16),
            V((NY - 1, slot, 128), BF16),
            V((NZ, slot, 128), BF16),
            pltpu.SemaphoreType.DMA((n,)),
            pltpu.SemaphoreType.DMA((n,)),
        ],
        compiler_params=pltpu.CompilerParams(
            collective_id=0, has_side_effects=True, vmem_limit_bytes=40 * 1024 * 1024
        ),
        name="conv_and_grad",
    )(
        clip_frames,
        conv_weight.reshape(3, 3, 384, 128),
        conv_bias.reshape(1, 128),
        out_grad,
        prev_group,
    )
    weight_grad = gathered[:, :, :part].astype(F32).reshape(3, 3, 3, 128, 128)
    return (conv_out, weight_grad)


def solution(mesh):
    return jax.shard_map(
        body,
        mesh=mesh,
        in_specs=(
            P("clip", "tile", None, None),
            P(),
            P(),
            P("clip", "tile", None, None),
            P("clip"),
        ),
        out_specs=(P("clip", "tile", None, None), P()),
        check_vma=False,
    )
```

time: 613 us -> 84.3 us (0.14)
  waiting for transfers between devices: 561 us -> 0 us
  Pallas kernels: 0 us -> 77 us
  starting transfers between devices: 16.1 us -> 0 us
  between operations: 15.2 us -> 1.31 us
  matrix products: 7.72 us -> 0 us
    psum x1 -> x0, waiting for transfers between devices: 472 us -> none  [body(): summed = lax.psum(local_terms, ('clip', 'tile'))]
    all_gather x1 -> x0, waiting for transfers between devices: 85.6 us -> none  [body(): shards = lax.all_gather(tail, 'clip', axis=0, tiled=True)]
    pallas_call x0 -> x1, Pallas kernels: none -> 77 us  [body(): pl.pallas_call(functools.partial(kernel, factor), out_shape=(jax.ShapeDty...]
    ppermute x2 -> x0, starting transfers between devices: 16 us -> none  [the longest x1 14.1 us: with_halo(): lax.ppermute(tail, axis, [(i, (i + 1) % count) for i in range(ends)])]
    dot_general x18 -> x0, matrix products: 7.72 us -> none  [the longest x9 4.89 us: body(): jnp.dot(columns, weights[frame_tap, row_tap], preferred_element_type=jnp....]
  transfers between devices with their start and end apart: 4 -> 0, of which waited for: 3 -> 0; matrix products, arithmetic and copies ran while one was open for 1% -> 0% of each run, Pallas kernels for 0% -> 0%
where the time goes in v1:
time: 84.3 us; the launch traced here: 84.1 us
  Pallas kernels  77 us (91%)
  local copies, waits for them, and re-layouts  4.34 us (5%)
  other arithmetic  1.41 us (2%)
  between operations  1.31 us (2%)
    pallas_call x1, Pallas kernels, body(): pl.pallas_call(functools.partial(kernel, factor), out_shape=(jax.ShapeDty...  77 us
    unnamed x9, local copies, waits for them, and re-layouts  4.28 us

profile of v1, /device:TPU:1, one launch (start us, length us, event | category | flops | bytes accessed | tf_op | source)
XLA Modules:
  0.0 84.1 jit_solution(6544120856991859603)
XLA Ops:
  1.3 0.0 copy-start
  1.3 1.2 %copy-done = bf16[3,3,3,128,128]{4,3,2,1,0:T(8,128)(2,1)S(1)} copy-done((bf16[3,3,3,128,128]{4,3,2,1,0:T(8,128)(2,1)S(1)}, bf16[3,3,3,128,128]{4,3,2,1,0:T(8,128)(2,1)}, u32[]{:S(2)}) %copy-start) | copy-done | bytes 884760
  2.4 0.0 copy-start.1
  2.4 0.9 %copy-done.1 = bf16[4,2,64,128]{3,2,1,0:T(8,128)(2,1)S(1)} copy-done((bf16[4,2,64,128]{3,2,1,0:T(8,128)(2,1)S(1)}, bf16[4,2,64,128]{3,2,1,0:T(8,128)(2,1)}, u32[]{:S(2)}) %copy-start.1) | copy-done | bytes 131096
  3.4 0.0 copy-start.2
  3.4 0.9 %copy-done.2 = bf16[4,2,64,128]{3,2,1,0:T(8,128)(2,1)S(1)} copy-done((bf16[4,2,64,128]{3,2,1,0:T(8,128)(2,1)S(1)}, bf16[4,2,64,128]{3,2,1,0:T(8,128)(2,1)}, u32[]{:S(2)}) %copy-start.2) | copy-done | bytes 131096
  4.3 0.0 copy-start.3
  4.3 0.7 copy-done.3
  4.9 77.0 %conv_and_grad.1 = (bf16[4,2,64,128]{3,2,1,0:T(8,128)(2,1)S(1)}, bf16[2,4,512,128]{3,2,1,0:T(8,128)(2,1)S(1)}) custom-call(bf16[4,2,64,128]{3,2,1,0:T(8,128)(2,1)S(1)} %copy-done.1, bf16[3,3,384,128]{3,2,1,0:T(8,128)(2,1)S(1)} %bitcast.4, f32[1,128]{1,0:T(1,128)S(1)} %bitcast.5, bf16[4,2,64,128]{3,2,1,0:T(8,128)(2,1)S(1)} %copy-done.2, s32[1]{0:T(128)S(6)} %copy.8.prev), custom_call_target="tpu_custom_call" | custom-call | tf_op jit(solution)/shard_map/conv_and_grad/pallas_call | solution.py:291
  81.9 0.1 slice.3
  82.0 1.4 %convert.1 = f32[3,3,3,128,128]{4,3,2,1,0:T(8,128)} convert(bf16[3,3,3,128,128]{4,3,2,1,0:T(8,128)(2,1)S(1)} %bitcast.6) | non-fusion elementwise | flops 442368 | bytes 2654208 | tf_op jit(solution)/shard_map/reshape | solution.py:337
  83.4 0.7 copy.9
Async XLA Ops:
  1.3 1.2 %copy-start = (bf16[3,3,3,128,128]{4,3,2,1,0:T(8,128)(2,1)S(1)}, bf16[3,3,3,128,128]{4,3,2,1,0:T(8,128)(2,1)}, u32[]{:S(2)}) copy-start(bf16[3,3,3,128,128]{4,3,2,1,0:T(8,128)(2,1)} %param.6) | copy-start | bytes 2654212
  2.4 0.9 %copy-start.1 = (bf16[4,2,64,128]{3,2,1,0:T(8,128)(2,1)S(1)}, bf16[4,2,64,128]{3,2,1,0:T(8,128)(2,1)}, u32[]{:S(2)}) copy-start(bf16[4,2,64,128]{3,2,1,0:T(8,128)(2,1)} %frames.1) | copy-start | bytes 393220
  3.4 0.9 %copy-start.2 = (bf16[4,2,64,128]{3,2,1,0:T(8,128)(2,1)S(1)}, bf16[4,2,64,128]{3,2,1,0:T(8,128)(2,1)}, u32[]{:S(2)}) copy-start(bf16[4,2,64,128]{3,2,1,0:T(8,128)(2,1)} %grads.1) | copy-start | bytes 393220
  4.3 0.7 copy-start.3

commit v2 on v1

v2 whole, which is shorter than its diff:
```python
import functools
import math

import jax
import jax.numpy as jnp
from jax import lax
from jax.experimental import pallas as pl
from jax.experimental.pallas import tpu as pltpu
from jax.sharding import PartitionSpec as P

MESH = pl.DeviceIdType.MESH
NX, NZL, NZH, NY = 4, 4, 3, 8
NZ = NZH * NZL
F32, BF16 = jnp.float32, jnp.bfloat16


def sizes():
    half = 27 * 128 // 2
    part = half // NX
    slot = -(-part // (16 * NY)) * 16
    return half, part, slot


class Place:
    def __init__(self):
        clip, tile = lax.axis_index("clip"), lax.axis_index("tile")
        self.x, self.zl = clip % NX, clip // NX
        self.core, self.y, self.zh = tile % 2, (tile // 2) % NY, tile // (2 * NY)
        self.z = self.zh * NZL + self.zl
        self.clip, self.tile = clip, tile

    def at(self, x=None, y=None, z=None, core=None):
        x = self.x if x is None else x
        y = self.y if y is None else y
        z = self.z if z is None else z
        core = self.core if core is None else core
        return ((z % NZL) * NX + x, ((z // NZL) * NY + y) * 2 + core)


def kernel(
    factor, frames_hbm, weight_hbm, bias_hbm, grads_hbm, prev, out, gathered,
    frames, weight, bias, act, cat, turned, gext, acc,
    ids_x, ids_z, gx, gm, gz, zx, zm, zz,
    local, core_out, core_in, sum_a, x_out, x_in, y_out, y_in, z_buf,
    s_sem, r_sem, l_sem,
):
    half, part, slot = sizes()
    me = Place()
    tiles = 2 * NY * NZH
    up, down = (me.tile + tiles - 1) % tiles, (me.tile + 1) % tiles
    other = 1 - me.core
    core_peer = me.at(core=other)
    diag_tile = jnp.where(me.core == 0, up, down)
    pairs = NY // 2
    by_pair = sorted(range(pairs), key=lambda d: -min(d, pairs - d))
    my_pair, my_side = me.y // 2, me.y % 2
    sides = (my_side, 1 - my_side)
    by_z = sorted(range(1, NZ), key=lambda d: -min(d, NZ - d))
    xs = [(me.x + j) % NX for j in range(1, NX)]
    zls = [(me.zl + j) % NZL for j in range(1, NZL)]
    x_peers = [me.at(x=x) for x in xs]
    y_peer = {
        (d, r): me.at(y=(my_pair + d) % pairs * 2 + sides[r])
        for d in by_pair for r in range(2) if (d, r) != (0, 0)
    }
    z_peers = [me.at(z=(me.z + d) % NZ) for d in by_z]
    zl_peers = [me.at(z=me.zh * NZL + zl) for zl in zls]

    barrier = pltpu.get_barrier_semaphore()
    everyone = [core_peer, (me.clip, diag_tile), *x_peers, *y_peer.values(), *z_peers]
    for peer in everyone:
        pl.semaphore_signal(barrier, inc=1, device_id=peer, device_id_type=MESH)
    loads = [
        pltpu.make_async_copy(src, dst, l_sem.at[k])
        for k, (src, dst) in enumerate(
            ((frames_hbm, frames), (grads_hbm, gext.at[pl.ds(0, 512)]), (weight_hbm, weight), (bias_hbm, bias))
        )
    ]
    for load in loads:
        load.start()

    started = []

    def send(src, dst, peer):
        k = len(started)
        copy = pltpu.make_async_remote_copy(
            src_ref=src, dst_ref=dst, send_sem=s_sem.at[k], recv_sem=r_sem.at[k],
            device_id=peer, device_id_type=MESH,
        )
        copy.start()
        started.append(copy)
        return copy

    own_id = jnp.full((8, 128), prev[0], jnp.int32)
    ids_x[me.x] = own_id
    ids_z[me.zl] = own_id
    acc[...] = jnp.zeros((6, 128, 128), F32)
    pad = NY * slot - part
    if pad:
        core_out[:, part:] = jnp.zeros((NX, pad, 128), BF16)
        local[pl.ds(2 * half, pad)] = jnp.zeros((pad, 128), F32)
    loads[0].wait()
    for s in range(4):
        v = frames[s].astype(F32)
        act[s, 1:3] = (v / (1.0 + jnp.exp(-v))).astype(BF16)
    loads[1].wait()
    gx[me.x] = gext[0:256].reshape(2, 128, 128)
    pl.semaphore_wait(barrier, len(everyone))

    id_x = [send(ids_x.at[me.x], ids_x.at[me.x], peer) for peer in x_peers]
    g_first = [
        [send(gext.at[pl.ds(f * 128, 128)], gx.at[me.x, f], peer) for peer in x_peers]
        for f in range(2)
    ]
    halo_up = send(act.at[:, 1], act.at[:, 3], (me.clip, up))
    halo_down = send(act.at[:, 2], act.at[:, 0], (me.clip, down))
    id_z = [send(ids_z.at[me.zl], ids_z.at[me.zl], peer) for peer in zl_peers]

    for copy in id_x:
        copy.wait_recv()

    def g_message(target, f):
        total = jnp.zeros((128, 128), F32)
        for k in range(NX):
            chosen = (ids_x[k][0:1] == target * NX + me.x).astype(F32)
            total = total + gx[k, f].astype(F32) * chosen
        return total.astype(BF16)

    g_second = []
    for f in range(2):
        for copy in g_first[f]:
            copy.wait_recv()
        for j in range(NZL - 1):
            gm[j, f] = g_message(zls[j], f)
            g_second.append(send(gm.at[j, f], gz.at[j, f], zl_peers[j]))
    own_next = [g_message(me.zl, f).astype(F32) for f in range(2)]

    halo_up.wait_recv()
    halo_down.wait_recv()
    top = jnp.where(me.tile == 0, 0.0, 1.0).astype(F32)
    bottom = jnp.where(me.tile == tiles - 1, 0.0, 1.0).astype(F32)
    row_at = lax.broadcasted_iota(jnp.int32, (64, 128), 0)

    def widen(s, _):
        for r in range(4):
            v = act[s, r].astype(F32)
            if r == 0:
                v = v * top
            if r == 3:
                v = v * bottom
            left = jnp.where(row_at == 0, 0.0, pltpu.roll(v, 1, 0))
            right = jnp.where(row_at == 63, 0.0, pltpu.roll(v, 63, 0))
            cat[s, r, :, 0:128] = left.astype(BF16)
            cat[s, r, :, 128:256] = v.astype(BF16)
            cat[s, r, :, 256:384] = right.astype(BF16)
        return 0

    lax.fori_loop(0, 4, widen, 0)

    def turn(s, b):
        for e in range(3):
            block = cat[s, pl.ds(b, 2), :, e * 128 : (e + 1) * 128].reshape(128, 128)
            start = pl.multiple_of((b * 3 + e) * 128, 128)
            turned[s, pl.ds(start, 128), :] = block.T

    for s in range(4):
        lax.fori_loop(0, 3, lambda b, _, s=s: (turn(s, b), 0)[1], 0)

    def grad_of(a, frames_used, more):
        first = (2 - a) * 128

        def block(k, _):
            rows = pl.ds(pl.multiple_of(k * 384, 128), 384)
            at = pl.ds(pl.multiple_of(a * 1152 + k * 384, 128), 384)
            total = local[at] if more else jnp.zeros((384, 128), F32)
            for s in frames_used:
                total = total + jnp.dot(
                    turned[s, rows, :], gext[first + s * 128 : first + (s + 1) * 128],
                    preferred_element_type=F32,
                )
            local[at] = total
            return 0

        lax.fori_loop(0, 3, block, 0)

    grad_of(2, (0, 1, 2, 3), False)
    grad_of(1, (0, 1, 2), False)
    grad_of(0, (0, 1), False)

    loads[2].wait()
    loads[3].wait()

    def conv(a, _):
        for s in range(4):
            total = jnp.zeros((128, 128), F32)
            for b in range(3):
                total = total + jnp.dot(
                    cat[s, b : b + 2].reshape(128, 384), weight[a, b], preferred_element_type=F32
                )
            acc[s + 2 - a] = acc[s + 2 - a] + total
        return 0

    lax.fori_loop(0, 3, conv, 0)
    zx[me.x] = acc[4:6].reshape(256, 128).astype(BF16)
    z_first = [send(zx.at[me.x], zx.at[me.x], peer) for peer in x_peers]

    for copy in g_second:
        copy.wait_recv()
    for f in range(2):
        gn = own_next[f]
        for j in range(NZL - 1):
            gn = gn + gz[j, f].astype(F32)
        gext[512 + f * 128 : 640 + f * 128] = gn.astype(BF16)
    grad_of(1, (3,), True)
    grad_of(0, (2, 3), True)

    def pair_at(d):
        return pl.ds(pl.multiple_of((my_pair + d) % pairs * (2 * slot), 16), 2 * slot)

    def block_at(d, r):
        return pl.ds(
            pl.multiple_of(((my_pair + d) % pairs * 2 + sides[r]) * slot, 16), slot
        )

    for x in range(NX):
        core_out[x, 0:part] = local[
            pl.ds(pl.multiple_of(other * half + x * part, 16), part)
        ].astype(BF16)
    core_copies = []
    for d in by_pair:
        at = pair_at(d)
        core_copies.append(send(core_out.at[:, at], core_in.at[:, at], core_peer))

    x_copies = []
    for i, d in enumerate(by_pair):
        at = pair_at(d)
        core_copies[i].wait_recv()

        def both_cores(x):
            start = me.core * half + x * part + (my_pair + d) % pairs * (2 * slot)
            return local[pl.ds(pl.multiple_of(start, 16), 2 * slot)] + core_in[x, at].astype(F32)

        for j in range(NX - 1):
            x_out[j, at] = both_cores(xs[j]).astype(BF16)
        x_copies.append(
            [send(x_out.at[j, at], x_in.at[j, at], x_peers[j]) for j in range(NX - 1)]
        )
        sum_a[at] = both_cores(me.x)

    y_copies = {}
    for i, d in enumerate(by_pair):
        for copy in x_copies[i]:
            copy.wait_recv()
        for r in (1, 0):
            at = block_at(d, r)
            total = sum_a[at]
            for j in range(NX - 1):
                total = total + x_in[j, at].astype(F32)
            if (d, r) != (0, 0):
                k = 2 * d + r - 1
                y_out[k] = total.astype(BF16)
                y_copies[d, r] = send(y_out.at[k], y_in.at[k], y_peer[d, r])

    for copy in z_first + id_z:
        copy.wait_recv()

    def z_message(target):
        ids = ids_z[target][0:1]
        message = jnp.zeros((256, 128), F32)
        for k in range(NX):
            message = message + zx[k].astype(F32) * (ids == me.zl * NX + k).astype(F32)
        return message.astype(BF16)

    z_second = []
    for j in range(NZL - 1):
        zm[j] = z_message(zls[j])
        z_second.append(send(zm.at[j], zz.at[j], zl_peers[j]))
    zn = z_message(me.zl).astype(F32)

    for copy in y_copies.values():
        copy.wait_recv()
    for j in range(NY - 1):
        total = total + y_in[j].astype(F32)
    z_buf[me.z] = total.astype(BF16)

    z_copies = [send(z_buf.at[me.z], z_buf.at[me.z], peer) for peer in z_peers]

    for copy in z_second:
        copy.wait_recv()
    for j in range(NZL - 1):
        zn = zn + zz[j].astype(F32)
    acc[0:2] = acc[0:2] + zn.reshape(2, 128, 128)
    out[...] = (acc[0:4].reshape(512, 128) + bias[...]).astype(BF16).reshape(4, 2, 64, 128)

    for copy in z_copies:
        copy.wait_recv()
    total = z_buf[0].astype(F32)
    for k in range(1, NZ):
        total = total + z_buf[k].astype(F32)
    gathered[me.core, me.x, block_at(0, 0)] = (total * factor).astype(BF16)

    own = gathered.at[me.core, me.x, block_at(0, 0)]
    y_back = {key: send(own, own, y_peer[key]) for key in y_copies}
    x_back = []
    for d in reversed(by_pair):
        for r in range(2):
            if (d, r) != (0, 0):
                y_back[d, r].wait_recv()
        block = gathered.at[me.core, me.x, pair_at(pairs - d)]
        x_back.append([send(block, block, peer) for peer in x_peers])
    core_back = []
    for i, d in enumerate(reversed(by_pair)):
        for copy in x_back[i]:
            copy.wait_recv()
        block = gathered.at[me.core, :, pair_at(pairs - d)]
        core_back.append(send(block, block, core_peer))
    for copy in core_back:
        copy.wait_recv()
    for copy in started:
        copy.wait_send()


def n_copies():
    routing = 2 + 4 * (NX - 1) + 4 * (NZL - 1)
    scatter = NY // 2 + NY // 2 * (NX - 1) + (NY - 1)
    return routing + 2 * scatter + NZ - 1


def body(clip_frames, conv_weight, conv_bias, out_grad, prev_group):
    half, part, slot = sizes()
    factor = 1.0 / math.sqrt(
        4 * lax.axis_size("clip") * 2 * lax.axis_size("tile") * 64
    )
    hbm = pl.BlockSpec(memory_space=pltpu.HBM)
    V = pltpu.VMEM
    n = n_copies()
    conv_out, gathered = pl.pallas_call(
        functools.partial(kernel, factor),
        out_shape=(
            pltpu.VMEM((4, 2, 64, 128), BF16),
            pltpu.VMEM((2, NX, NY * slot, 128), BF16),
        ),
        in_specs=[hbm, hbm, hbm, hbm, pl.BlockSpec(memory_space=pltpu.SMEM)],
        out_specs=(pl.BlockSpec(memory_space=pltpu.VMEM),) * 2,
        scratch_shapes=[
            V((4, 2, 64, 128), BF16),
            V((3, 3, 384, 128), BF16),
            V((1, 128), F32),
            V((4, 4, 64, 128), BF16),
            V((4, 4, 64, 384), BF16),
            V((4, 1152, 128), BF16),
            V((768, 128), BF16),
            V((6, 128, 128), F32),
            V((NX, 8, 128), jnp.int32),
            V((NZL, 8, 128), jnp.int32),
            V((NX, 2, 128, 128), BF16),
            V((NZL, 2, 128, 128), BF16),
            V((NZL, 2, 128, 128), BF16),
            V((NX, 256, 128), BF16),
            V((NZL, 256, 128), BF16),
            V((NZL, 256, 128), BF16),
            V((2 * half - part + NY * slot, 128), F32),
            V((NX, NY * slot, 128), BF16),
            V((NX, NY * slot, 128), BF16),
            V((NY * slot, 128), F32),
            V((NX - 1, NY * slot, 128), BF16),
            V((NX - 1, NY * slot, 128), BF16),
            V((NY - 1, slot, 128), BF16),
            V((NY - 1, slot, 128), BF16),
            V((NZ, slot, 128), BF16),
            pltpu.SemaphoreType.DMA((n,)),
            pltpu.SemaphoreType.DMA((n,)),
            pltpu.SemaphoreType.DMA((7,)),
        ],
        compiler_params=pltpu.CompilerParams(
            collective_id=0, has_side_effects=True, vmem_limit_bytes=58000 * 1024
        ),
        name="conv_and_grad",
    )(
        clip_frames,
        conv_weight.reshape(3, 3, 384, 128),
        conv_bias.reshape(1, 128),
        out_grad.reshape(512, 128),
        prev_group,
    )
    weight_grad = gathered[:, :, :part].astype(F32).reshape(3, 3, 3, 128, 128)
    return (conv_out, weight_grad)


def solution(mesh):
    return jax.shard_map(
        body,
        mesh=mesh,
        in_specs=(
            P("clip", "tile", None, None),
            P(),
            P(),
            P("clip", "tile", None, None),
            P("clip"),
        ),
        out_specs=(P("clip", "tile", None, None), P()),
        check_vma=False,
    )
```

time: 84.3 us -> 71.7 us (0.85)
  Pallas kernels: 77 us -> 68.2 us
  local copies, waits for them, and re-layouts: 4.34 us -> 0.72 us
    pallas_call x1, Pallas kernels: 77 us -> 68.2 us  [body(): pl.pallas_call(functools.partial(kernel, factor), out_shape=(pltpu.VMEM((...]
    unnamed x9 -> x1, local copies, waits for them, and re-layouts: 4.28 us -> 0.66 us
where the time goes in v2:
time: 71.7 us; the launch traced here: 71.6 us
  Pallas kernels  68.2 us (95%)
  other arithmetic  1.41 us (2%)
  between operations  1.29 us (2%)
  local copies, waits for them, and re-layouts  0.72 us (1%)
    pallas_call x1, Pallas kernels, body(): pl.pallas_call(functools.partial(kernel, factor), out_shape=(pltpu.VMEM((...  68.2 us

profile of v2, /device:TPU:1, one launch (start us, length us, event | category | flops | bytes accessed | tf_op | source)
XLA Modules:
  0.0 71.6 jit_solution(8933262602159504555)
XLA Ops:
  1.3 68.2 %conv_and_grad.1 = (bf16[4,2,64,128]{3,2,1,0:T(8,128)(2,1)S(1)}, bf16[2,4,512,128]{3,2,1,0:T(8,128)(2,1)S(1)}) custom-call(bf16[4,2,64,128]{3,2,1,0:T(8,128)(2,1)} %frames_hbm.1, bf16[3,3,384,128]{3,2,1,0:T(8,128)(2,1)} %bitcast.6, f32[1,128]{1,0:T(1,128)} %bitcast.8, bf16[512,128]{1,0:T(8,128)(2,1)} %bitcast.7, s32[1]{0:T(128)S(6)} %copy.9.prev), custom_call_target="tpu_custom_call" | custom-call | tf_op jit(solution)/shard_map/conv_and_grad/pallas_call | solution.py:337
  69.4 0.7 copy.8
  70.1 0.1 slice.3
  70.2 1.4 %convert.1 = f32[3,3,3,128,128]{4,3,2,1,0:T(8,128)} convert(bf16[3,3,3,128,128]{4,3,2,1,0:T(8,128)(2,1)S(1)} %bitcast.5) | non-fusion elementwise | flops 442368 | bytes 2654208 | tf_op jit(solution)/shard_map/reshape | solution.py:386

commit v3 on v2

--- a/solution.py
+++ b/solution.py
@@ -40,9 +40,9 @@
 def kernel(
     factor, frames_hbm, weight_hbm, bias_hbm, grads_hbm, prev, out, gathered,
     frames, weight, bias, act, cat, turned, gext, acc,
-    ids_x, ids_z, gx, gm, gz, zx, zm, zz,
+    ids_x, ids_z, gx, gm, gz, hz, hm, hx, zx, zm, zz,
     local, core_out, core_in, sum_a, x_out, x_in, y_out, y_in, z_buf,
-    s_sem, r_sem, l_sem,
+    s_sem, r_sem, l_sem, round_1, round_2,
 ):
     half, part, slot = sizes()
     me = Place()
@@ -67,8 +67,10 @@
     zl_peers = [me.at(z=me.zh * NZL + zl) for zl in zls]
 
     barrier = pltpu.get_barrier_semaphore()
-    everyone = [core_peer, (me.clip, diag_tile), *x_peers, *y_peer.values(), *z_peers]
-    for peer in everyone:
+    near = [core_peer, (me.clip, diag_tile), *x_peers, *zl_peers]
+    near += [me.at(y=(me.y + d) % NY) for d in (1, NY - 1, 2, NY - 2) if d % NY]
+    near += [me.at(z=(me.z + d) % NZ) for d in (1, NZ - 1, 2, NZ - 2) if d % NZ]
+    for peer in near:
         pl.semaphore_signal(barrier, inc=1, device_id=peer, device_id_type=MESH)
     loads = [
         pltpu.make_async_copy(src, dst, l_sem.at[k])
@@ -100,71 +102,83 @@
         core_out[:, part:] = jnp.zeros((NX, pad, 128), BF16)
         local[pl.ds(2 * half, pad)] = jnp.zeros((pad, 128), F32)
     loads[0].wait()
-    for s in range(4):
-        v = frames[s].astype(F32)
-        act[s, 1:3] = (v / (1.0 + jnp.exp(-v))).astype(BF16)
+    row_at = lax.broadcasted_iota(jnp.int32, (64, 128), 0)
+
+    def widen(s, r, v):
+        left = jnp.where(row_at == 0, 0.0, pltpu.roll(v, 1, 0))
+        right = jnp.where(row_at == 63, 0.0, pltpu.roll(v, 63, 0))
+        cat[s, r, :, 0:128] = left.astype(BF16)
+        cat[s, r, :, 128:256] = v.astype(BF16)
+        cat[s, r, :, 256:384] = right.astype(BF16)
+
+    def turn(s, b):
+        for e in range(3):
+            block = cat[s, b : b + 2, :, e * 128 : (e + 1) * 128].reshape(128, 128)
+            start = (b * 3 + e) * 128
+            turned[s, start : start + 128, :] = block.T
+
+    def activate(s, _):
+        for r in (1, 2):
+            v = frames[s, r - 1].astype(F32)
+            active = (v / (1.0 + jnp.exp(-v))).astype(BF16)
+            act[s, r] = active
+            widen(s, r, active.astype(F32))
+        turn(s, 1)
+        return 0
+
+    lax.fori_loop(0, 4, activate, 0)
     loads[1].wait()
-    gx[me.x] = gext[0:256].reshape(2, 128, 128)
-    pl.semaphore_wait(barrier, len(everyone))
+    gx[me.x] = gext[0:128]
+    hz[me.zl] = gext[128:256]
+    pl.semaphore_wait(barrier, len(near))
+    for peer in near:
+        pl.semaphore_signal(round_1, inc=1, device_id=peer, device_id_type=MESH)
 
     id_x = [send(ids_x.at[me.x], ids_x.at[me.x], peer) for peer in x_peers]
-    g_first = [
-        [send(gext.at[pl.ds(f * 128, 128)], gx.at[me.x, f], peer) for peer in x_peers]
-        for f in range(2)
-    ]
+    id_z = [send(ids_z.at[me.zl], ids_z.at[me.zl], peer) for peer in zl_peers]
+    g_first = [send(gext.at[pl.ds(0, 128)], gx.at[me.x], peer) for peer in x_peers]
+    h_first = [send(gext.at[pl.ds(128, 128)], hz.at[me.zl], peer) for peer in zl_peers]
     halo_up = send(act.at[:, 1], act.at[:, 3], (me.clip, up))
     halo_down = send(act.at[:, 2], act.at[:, 0], (me.clip, down))
-    id_z = [send(ids_z.at[me.zl], ids_z.at[me.zl], peer) for peer in zl_peers]
-
-    for copy in id_x:
-        copy.wait_recv()
-
-    def g_message(target, f):
-        total = jnp.zeros((128, 128), F32)
-        for k in range(NX):
-            chosen = (ids_x[k][0:1] == target * NX + me.x).astype(F32)
-            total = total + gx[k, f].astype(F32) * chosen
-        return total.astype(BF16)
-
+
+    def chosen(items, ids, target, number):
+        message = jnp.zeros(items.shape[1:], F32)
+        for k in range(number):
+            message = message + items[k].astype(F32) * (ids[k][0:1] == target).astype(F32)
+        return message.astype(BF16)
+
+    for copy in id_x + g_first:
+        copy.wait_recv()
     g_second = []
-    for f in range(2):
-        for copy in g_first[f]:
-            copy.wait_recv()
-        for j in range(NZL - 1):
-            gm[j, f] = g_message(zls[j], f)
-            g_second.append(send(gm.at[j, f], gz.at[j, f], zl_peers[j]))
-    own_next = [g_message(me.zl, f).astype(F32) for f in range(2)]
+    for j in range(NZL - 1):
+        gm[j] = chosen(gx, ids_x, zls[j] * NX + me.x, NX)
+        g_second.append(send(gm.at[j], gz.at[j], zl_peers[j]))
+    pl.semaphore_wait(round_1, len(near))
+    for peer in near:
+        pl.semaphore_signal(round_2, inc=1, device_id=peer, device_id_type=MESH)
+    for copy in id_z + h_first:
+        copy.wait_recv()
+    h_second = []
+    for j in range(NX - 1):
+        hm[j] = chosen(hz, ids_z, me.zl * NX + xs[j], NZL)
+        h_second.append(send(hm.at[j], hx.at[j], x_peers[j]))
+    own_next = [
+        chosen(items, ids, me.clip, number).astype(F32)
+        for items, ids, number in ((gx, ids_x, NX), (hz, ids_z, NZL))
+    ]
 
     halo_up.wait_recv()
     halo_down.wait_recv()
     top = jnp.where(me.tile == 0, 0.0, 1.0).astype(F32)
     bottom = jnp.where(me.tile == tiles - 1, 0.0, 1.0).astype(F32)
-    row_at = lax.broadcasted_iota(jnp.int32, (64, 128), 0)
-
-    def widen(s, _):
-        for r in range(4):
-            v = act[s, r].astype(F32)
-            if r == 0:
-                v = v * top
-            if r == 3:
-                v = v * bottom
-            left = jnp.where(row_at == 0, 0.0, pltpu.roll(v, 1, 0))
-            right = jnp.where(row_at == 63, 0.0, pltpu.roll(v, 63, 0))
-            cat[s, r, :, 0:128] = left.astype(BF16)
-            cat[s, r, :, 128:256] = v.astype(BF16)
-            cat[s, r, :, 256:384] = right.astype(BF16)
+
+    def widen_halo(s, _):
+        widen(s, 0, act[s, 0].astype(F32) * top)
+        widen(s, 3, act[s, 3].astype(F32) * bottom)
         return 0
 
-    lax.fori_loop(0, 4, widen, 0)
-
-    def turn(s, b):
-        for e in range(3):
-            block = cat[s, pl.ds(b, 2), :, e * 128 : (e + 1) * 128].reshape(128, 128)
-            start = pl.multiple_of((b * 3 + e) * 128, 128)
-            turned[s, pl.ds(start, 128), :] = block.T
-
-    for s in range(4):
-        lax.fori_loop(0, 3, lambda b, _, s=s: (turn(s, b), 0)[1], 0)
+    lax.fori_loop(0, 4, widen_halo, 0)
+    lax.fori_loop(0, 4, lambda s, _: (turn(s, 0), turn(s, 2), 0)[2], 0)
 
     def grad_of(a, frames_used, more):
         first = (2 - a) * 128
@@ -187,29 +201,12 @@
     grad_of(1, (0, 1, 2), False)
     grad_of(0, (0, 1), False)
 
-    loads[2].wait()
-    loads[3].wait()
-
-    def conv(a, _):
-        for s in range(4):
-            total = jnp.zeros((128, 128), F32)
-            for b in range(3):
-                total = total + jnp.dot(
-                    cat[s, b : b + 2].reshape(128, 384), weight[a, b], preferred_element_type=F32
-                )
-            acc[s + 2 - a] = acc[s + 2 - a] + total
-        return 0
-
-    lax.fori_loop(0, 3, conv, 0)
-    zx[me.x] = acc[4:6].reshape(256, 128).astype(BF16)
-    z_first = [send(zx.at[me.x], zx.at[me.x], peer) for peer in x_peers]
-
-    for copy in g_second:
-        copy.wait_recv()
-    for f in range(2):
+    for copy in g_second + h_second:
+        copy.wait_recv()
+    for f, pieces, number in ((0, gz, NZL), (1, hx, NX)):
         gn = own_next[f]
-        for j in range(NZL - 1):
-            gn = gn + gz[j, f].astype(F32)
+        for j in range(number - 1):
+            gn = gn + pieces[j].astype(F32)
         gext[512 + f * 128 : 640 + f * 128] = gn.astype(BF16)
     grad_of(1, (3,), True)
     grad_of(0, (2, 3), True)
@@ -247,6 +244,7 @@
         )
         sum_a[at] = both_cores(me.x)
 
+    pl.semaphore_wait(round_2, len(near))
     y_copies = {}
     for i, d in enumerate(by_pair):
         for copy in x_copies[i]:
@@ -261,7 +259,32 @@
                 y_out[k] = total.astype(BF16)
                 y_copies[d, r] = send(y_out.at[k], y_in.at[k], y_peer[d, r])
 
-    for copy in z_first + id_z:
+    loads[2].wait()
+    loads[3].wait()
+
+    def conv(a, _):
+        for s in range(4):
+            total = jnp.zeros((128, 128), F32)
+            for b in range(3):
+                total = total + jnp.dot(
+                    cat[s, b : b + 2].reshape(128, 384), weight[a, b], preferred_element_type=F32
+                )
+            acc[s + 2 - a] = acc[s + 2 - a] + total
+        return 0
+
+    lax.fori_loop(0, 3, conv, 0)
+    zx[me.x] = acc[4:6].reshape(256, 128).astype(BF16)
+    z_first = [send(zx.at[me.x], zx.at[me.x], peer) for peer in x_peers]
+
+    for copy in y_copies.values():
+        copy.wait_recv()
+    for j in range(NY - 1):
+        total = total + y_in[j].astype(F32)
+    z_buf[me.z] = total.astype(BF16)
+
+    z_copies = [send(z_buf.at[me.z], z_buf.at[me.z], peer) for peer in z_peers]
+
+    for copy in z_first:
         copy.wait_recv()
 
     def z_message(target):
@@ -271,26 +294,9 @@
             message = message + zx[k].astype(F32) * (ids == me.zl * NX + k).astype(F32)
         return message.astype(BF16)
 
-    z_second = []
     for j in range(NZL - 1):
         zm[j] = z_message(zls[j])
-        z_second.append(send(zm.at[j], zz.at[j], zl_peers[j]))
     zn = z_message(me.zl).astype(F32)
-
-    for copy in y_copies.values():
-        copy.wait_recv()
-    for j in range(NY - 1):
-        total = total + y_in[j].astype(F32)
-    z_buf[me.z] = total.astype(BF16)
-
-    z_copies = [send(z_buf.at[me.z], z_buf.at[me.z], peer) for peer in z_peers]
-
-    for copy in z_second:
-        copy.wait_recv()
-    for j in range(NZL - 1):
-        zn = zn + zz[j].astype(F32)
-    acc[0:2] = acc[0:2] + zn.reshape(2, 128, 128)
-    out[...] = (acc[0:4].reshape(512, 128) + bias[...]).astype(BF16).reshape(4, 2, 64, 128)
 
     for copy in z_copies:
         copy.wait_recv()
@@ -301,6 +307,7 @@
 
     own = gathered.at[me.core, me.x, block_at(0, 0)]
     y_back = {key: send(own, own, y_peer[key]) for key in y_copies}
+    z_second = [send(zm.at[j], zz.at[j], zl_peers[j]) for j in range(NZL - 1)]
     x_back = []
     for d in reversed(by_pair):
         for r in range(2):
@@ -308,6 +315,13 @@
                 y_back[d, r].wait_recv()
         block = gathered.at[me.core, me.x, pair_at(pairs - d)]
         x_back.append([send(block, block, peer) for peer in x_peers])
+    for copy in z_second:
+        copy.wait_recv()
+    for j in range(NZL - 1):
+        zn = zn + zz[j].astype(F32)
+    acc[0:2] = acc[0:2] + zn.reshape(2, 128, 128)
+    out[...] = (acc[0:4].reshape(512, 128) + bias[...]).astype(BF16).reshape(4, 2, 64, 128)
+
     core_back = []
     for i, d in enumerate(reversed(by_pair)):
         for copy in x_back[i]:
@@ -353,9 +367,12 @@
             V((6, 128, 128), F32),
             V((NX, 8, 128), jnp.int32),
             V((NZL, 8, 128), jnp.int32),
-            V((NX, 2, 128, 128), BF16),
-            V((NZL, 2, 128, 128), BF16),
-            V((NZL, 2, 128, 128), BF16),
+            V((NX, 128, 128), BF16),
+            V((NZL, 128, 128), BF16),
+            V((NZL, 128, 128), BF16),
+            V((NZL, 128, 128), BF16),
+            V((NX, 128, 128), BF16),
+            V((NX, 128, 128), BF16),
             V((NX, 256, 128), BF16),
             V((NZL, 256, 128), BF16),
             V((NZL, 256, 128), BF16),
@@ -371,6 +388,8 @@
             pltpu.SemaphoreType.DMA((n,)),
             pltpu.SemaphoreType.DMA((n,)),
             pltpu.SemaphoreType.DMA((7,)),
+            pltpu.SemaphoreType.REGULAR,
+            pltpu.SemaphoreType.REGULAR,
         ],
         compiler_params=pltpu.CompilerParams(
             collective_id=0, has_side_effects=True, vmem_limit_bytes=58000 * 1024

time: 71.7 us -> 69 us (0.962)
  Pallas kernels: 68.2 us -> 65.4 us
    pallas_call x1, Pallas kernels: 68.2 us -> 65.4 us  [body(): pl.pallas_call(functools.partial(kernel, factor), out_shape=(pltpu.VMEM((...]
where the time goes in v3:
time: 69 us; the launch traced here: 68.9 us
  Pallas kernels  65.4 us (95%)
  other arithmetic  1.41 us (2%)
  between operations  1.29 us (2%)
  local copies, waits for them, and re-layouts  0.72 us (1%)
    pallas_call x1, Pallas kernels, body(): pl.pallas_call(functools.partial(kernel, factor), out_shape=(pltpu.VMEM((...  65.4 us
    reshape x1, other arithmetic, body(): weight_grad = gathered[:, :, :part].astype(F32).reshape(3, 3, 3, 128, 128)  1.41 us

profile of v3, /device:TPU:1, one launch (start us, length us, event | category | flops | bytes accessed | tf_op | source)
XLA Modules:
  0.0 68.9 jit_solution(5223257112141445999)
XLA Ops:
  1.3 65.4 %conv_and_grad.1 = (bf16[4,2,64,128]{3,2,1,0:T(8,128)(2,1)S(1)}, bf16[2,4,512,128]{3,2,1,0:T(8,128)(2,1)S(1)}) custom-call(bf16[4,2,64,128]{3,2,1,0:T(8,128)(2,1)} %frames_hbm.1, bf16[3,3,384,128]{3,2,1,0:T(8,128)(2,1)} %bitcast.6, f32[1,128]{1,0:T(1,128)} %bitcast.8, bf16[512,128]{1,0:T(8,128)(2,1)} %bitcast.7, s32[1]{0:T(128)S(6)} %copy.9.prev), custom_call_target="tpu_custom_call" | custom-call | tf_op jit(solution)/shard_map/conv_and_grad/pallas_call | solution.py:351
  66.7 0.7 copy.8
  67.4 0.1 slice.3
  67.4 1.4 %convert.1 = f32[3,3,3,128,128]{4,3,2,1,0:T(8,128)} convert(bf16[3,3,3,128,128]{4,3,2,1,0:T(8,128)(2,1)S(1)} %bitcast.5) | non-fusion elementwise | flops 442368 | bytes 2654208 | tf_op jit(solution)/shard_map/reshape | solution.py:405

commit v4 on v3

--- a/solution.py
+++ b/solution.py
@@ -35,6 +35,24 @@
         z = self.z if z is None else z
         core = self.core if core is None else core
         return ((z % NZL) * NX + x, ((z // NZL) * NY + y) * 2 + core)
+
+
+class Either:
+    def __init__(self, first, when_first, when_not):
+        self.first, self.when_first, self.when_not = first, when_first, when_not
+
+    def both(self, act):
+        pl.when(self.first)(lambda: act(self.when_first))
+        pl.when(jnp.logical_not(self.first))(lambda: act(self.when_not))
+
+    def start(self):
+        self.both(lambda copy: copy.start())
+
+    def wait_recv(self):
+        self.both(lambda copy: copy.wait_recv())
+
+    def wait_send(self):
+        self.both(lambda copy: copy.wait_send())
 
 
 def kernel(
@@ -56,7 +74,8 @@
     my_pair, my_side = me.y // 2, me.y % 2
     sides = (my_side, 1 - my_side)
     by_z = sorted(range(1, NZ), key=lambda d: -min(d, NZ - d))
-    xs = [(me.x + j) % NX for j in range(1, NX)]
+    by_x = sorted(range(1, NX), key=lambda d: -min(d, NX - d))
+    xs = [(me.x + d) % NX for d in by_x]
     zls = [(me.zl + j) % NZL for j in range(1, NZL)]
     x_peers = [me.at(x=x) for x in xs]
     y_peer = {
@@ -82,6 +101,7 @@
         load.start()
 
     started = []
+    sent = [0]
 
     def send(src, dst, peer):
         k = len(started)
@@ -93,13 +113,36 @@
         started.append(copy)
         return copy
 
+    def send_pair(src_of, dst_of, d, peer):
+        k = len(started)
+        pair = (my_pair + d) % pairs
+        copies = []
+        for rows in (part - (pairs - 1) * 2 * slot, 2 * slot):
+            at = pl.ds(pl.multiple_of(pair * (2 * slot), 16), rows)
+            copies.append(
+                pltpu.make_async_remote_copy(
+                    src_ref=src_of(at), dst_ref=dst_of(at), send_sem=s_sem.at[k],
+                    recv_sem=r_sem.at[k], device_id=peer, device_id_type=MESH,
+                )
+            )
+        copy = Either(pair == pairs - 1, *copies)
+        copy.start()
+        started.append(copy)
+        return copy
+
+    def wait_sent(count):
+        for copy in started[sent[0] : count]:
+            copy.wait_send()
+        sent[0] = count
+
     own_id = jnp.full((8, 128), prev[0], jnp.int32)
     ids_x[me.x] = own_id
     ids_z[me.zl] = own_id
     acc[...] = jnp.zeros((6, 128, 128), F32)
     pad = NY * slot - part
     if pad:
-        core_out[:, part:] = jnp.zeros((NX, pad, 128), BF16)
+        core_in[:, part:] = jnp.zeros((NX, pad, 128), BF16)
+        x_in[:, part:] = jnp.zeros((NX - 1, pad, 128), BF16)
         local[pl.ds(2 * half, pad)] = jnp.zeros((pad, 128), F32)
     loads[0].wait()
     row_at = lax.broadcasted_iota(jnp.int32, (64, 128), 0)
@@ -225,8 +268,9 @@
         ].astype(BF16)
     core_copies = []
     for d in by_pair:
-        at = pair_at(d)
-        core_copies.append(send(core_out.at[:, at], core_in.at[:, at], core_peer))
+        core_copies.append(
+            send_pair(lambda at: core_out.at[:, at], lambda at: core_in.at[:, at], d, core_peer)
+        )
 
     x_copies = []
     for i, d in enumerate(by_pair):
@@ -240,7 +284,12 @@
         for j in range(NX - 1):
             x_out[j, at] = both_cores(xs[j]).astype(BF16)
         x_copies.append(
-            [send(x_out.at[j, at], x_in.at[j, at], x_peers[j]) for j in range(NX - 1)]
+            [
+                send_pair(
+                    lambda at, j=j: x_out.at[j, at], lambda at, j=j: x_in.at[j, at], d, x_peers[j]
+                )
+                for j in range(NX - 1)
+            ]
         )
         sum_a[at] = both_cores(me.x)
 
@@ -282,6 +331,7 @@
         total = total + y_in[j].astype(F32)
     z_buf[me.z] = total.astype(BF16)
 
+    before_z = len(started)
     z_copies = [send(z_buf.at[me.z], z_buf.at[me.z], peer) for peer in z_peers]
 
     for copy in z_first:
@@ -298,6 +348,7 @@
         zm[j] = z_message(zls[j])
     zn = z_message(me.zl).astype(F32)
 
+    wait_sent(before_z)
     for copy in z_copies:
         copy.wait_recv()
     total = z_buf[0].astype(F32)
@@ -313,8 +364,10 @@
         for r in range(2):
             if (d, r) != (0, 0):
                 y_back[d, r].wait_recv()
-        block = gathered.at[me.core, me.x, pair_at(pairs - d)]
-        x_back.append([send(block, block, peer) for peer in x_peers])
+        def block_of(at):
+            return gathered.at[me.core, me.x, at]
+
+        x_back.append([send_pair(block_of, block_of, pairs - d, peer) for peer in x_peers])
     for copy in z_second:
         copy.wait_recv()
     for j in range(NZL - 1):
@@ -326,12 +379,30 @@
     for i, d in enumerate(reversed(by_pair)):
         for copy in x_back[i]:
             copy.wait_recv()
-        block = gathered.at[me.core, :, pair_at(pairs - d)]
-        core_back.append(send(block, block, core_peer))
+        def side_of(at):
+            return gathered.at[me.core, :, at]
+
+        core_back.append(send_pair(side_of, side_of, pairs - d, core_peer))
+    wait_sent(len(started) - len(core_back))
     for copy in core_back:
         copy.wait_recv()
-    for copy in started:
-        copy.wait_send()
+    wait_sent(len(started))
+
+
+def widen_result(conv, gathered, conv_hbm, grad_hbm, wide, sem):
+    part = wide.shape[2]
+    copies = [pltpu.make_async_copy(conv, conv_hbm, sem.at[2 * NX])]
+    copies[0].start()
+    for core in range(2):
+        for x in range(NX):
+            wide[core, x] = gathered[core, x, 0:part].astype(F32)
+            copy = pltpu.make_async_copy(
+                wide.at[core, x], grad_hbm.at[core, x], sem.at[core * NX + x]
+            )
+            copy.start()
+            copies.append(copy)
+    for copy in copies:
+        copy.wait()
 
 
 def n_copies():
@@ -402,8 +473,23 @@
         out_grad.reshape(512, 128),
         prev_group,
     )
-    weight_grad = gathered[:, :, :part].astype(F32).reshape(3, 3, 3, 128, 128)
-    return (conv_out, weight_grad)
+    vmem = pl.BlockSpec(memory_space=pltpu.VMEM)
+    conv_out, weight_grad = pl.pallas_call(
+        widen_result,
+        out_shape=(
+            jax.ShapeDtypeStruct((4, 2, 64, 128), BF16),
+            jax.ShapeDtypeStruct((2, NX, part, 128), F32),
+        ),
+        in_specs=[vmem, vmem],
+        out_specs=(hbm, hbm),
+        scratch_shapes=[
+            V((2, NX, part, 128), F32),
+            pltpu.SemaphoreType.DMA((2 * NX + 1,)),
+        ],
+        compiler_params=pltpu.CompilerParams(vmem_limit_bytes=16 * 1024 * 1024),
+        name="widen_result",
+    )(conv_out, gathered)
+    return (conv_out, weight_grad.reshape(3, 3, 3, 128, 128))
 
 
 def solution(mesh):

time: 69 us -> 66.1 us (0.958)
  other arithmetic: 1.41 us -> 0 us
  Pallas kernels: 65.4 us -> 64.6 us
  local copies, waits for them, and re-layouts: 0.72 us -> 0 us
    pallas_call x1, Pallas kernels: 65.4 us -> 63.3 us  [body(): pl.pallas_call(functools.partial(kernel, factor), out_shape=(pltpu.VMEM((...]
    reshape x1 -> x0, other arithmetic: 1.41 us -> none  [body(): weight_grad = gathered[:, :, :part].astype(F32).reshape(3, 3, 3, 128, 128)]
    pallas_call x0 -> x1, Pallas kernels: none -> 1.32 us  [body(): pl.pallas_call(widen_result, out_shape=(jax.ShapeDtypeStruct((4, 2, 64, 1...]
where the time goes in v4:
time: 66.1 us; the launch traced here: 65.9 us
  Pallas kernels  64.6 us (98%)
  between operations  1.29 us (2%)
    pallas_call x1, Pallas kernels, body(): pl.pallas_call(functools.partial(kernel, factor), out_shape=(pltpu.VMEM((...  63.3 us

profile of v4, /device:TPU:1, one launch (start us, length us, event | category | flops | bytes accessed | tf_op | source)
XLA Modules:
  0.0 65.9 jit_solution(5415280256201784622)
XLA Ops:
  1.3 63.3 %conv_and_grad.1 = (bf16[4,2,64,128]{3,2,1,0:T(8,128)(2,1)S(1)}, bf16[2,4,512,128]{3,2,1,0:T(8,128)(2,1)S(1)}) custom-call(bf16[4,2,64,128]{3,2,1,0:T(8,128)(2,1)} %frames_hbm.1, bf16[3,3,384,128]{3,2,1,0:T(8,128)(2,1)} %bitcast.4, f32[1,128]{1,0:T(1,128)} %bitcast.6, bf16[512,128]{1,0:T(8,128)(2,1)} %bitcast.5, s32[1]{0:T(128)S(6)} %copy.7.prev), custom_call_target="tpu_custom_call" | custom-call | tf_op jit(solution)/shard_map/conv_and_grad/pallas_call | solution.py:422
  64.6 1.3 %widen_result.1 = (bf16[4,2,64,128]{3,2,1,0:T(8,128)(2,1)}, f32[2,4,432,128]{3,2,1,0:T(8,128)}) custom-call(bf16[4,2,64,128]{3,2,1,0:T(8,128)(2,1)S(1)} %get-tuple-element.6.conv, bf16[2,4,512,128]{3,2,1,0:T(8,128)(2,1)S(1)} %get-tuple-element.7.gathered), custom_call_target="tpu_custom_call" | custom-call | tf_op jit(solution)/shard_map/widen_result/pallas_call | solution.py:477
